TPU v7x, 128 devices: a whole 4x4x4 slice. The times are simulated.
128 devices in a mesh: dp: 16 (over y, z), tensor: 8 (over x, core).
Axes of the slice: x: 4, y: 4, z: 4, core: 2. Of those that a mesh axis runs over, the one named last changes fastest.
Arguments:
- residual: bfloat16 [2048, 8192], P('dp', 'tensor'), may hold values from -6 to 6
- partials: bfloat16 [8, 2048, 8192], P('tensor', 'dp'), may hold values from -4 to 4
- low_features: bfloat16 [2048, 8192], P('dp', 'tensor'), may hold values from -6 to 6
- mid_features: bfloat16 [2048, 8192], P('dp', 'tensor'), may hold values from -6 to 6
- join_weight: bfloat16 [3, 8192, 8192], P(None, 'tensor', 'dp'), may hold values from -0.0390625 to 0.0390625
- lengths: int32 [16, 5], replicated, may hold values from 16 to 32, as said below
- shard_of: int32 [16, 5], replicated, may hold values from 0 to 15, as said below
- joined_cotangent: bfloat16 [2048, 8192], P('tensor', 'dp'), may hold values from -0.19921875 to 0.19921875
Outputs:
- routed_rows: bfloat16 [16, 16, 32, 8192], P('dp', 'tensor')
- join_grad: float32 [3, 8192, 8192], P(None, 'tensor', 'dp')
Inputs may be any that keep to these rules, and one draw needn't show every extreme that they name: Row p holds the lengths of pack p's 5 conversations in token order; each row sums to 128 and its largest entry is exactly 32. `shard_of`: the conversations of one pack go to distinct draft shards, and every pack sends one of its conversations of length 32 to one common shard (a pack may hold more than one conversation of length 32; only one of them goes to the common shard).
All inputs are finite; a program needn't handle non-finite values.
Results may differ from a plain program's by a relative error of at most 0.015.
Values may be sent and summed in bfloat16 or wider, within the bound.
A program may use at most 128 MiB of HBM per device.

v0:
```python
import jax
import jax.numpy as jnp
from jax import lax
from jax.sharding import PartitionSpec as P


def build_slots(block, lengths, shard_of, shard_count, longest, pack_tokens):
    starts = jnp.cumsum(lengths, axis=1) - lengths
    shards = jnp.arange(shard_count, dtype=jnp.int32)
    match = (shard_of[None, :, :] == shards[:, None, None]).astype(jnp.int32)
    first = jnp.sum(match * starts[None, :, :], axis=2)
    count = jnp.sum(match * lengths[None, :, :], axis=2)
    offsets = jnp.arange(longest, dtype=jnp.int32)
    packs = jnp.arange(lengths.shape[0], dtype=jnp.int32)
    source = packs[None, :, None] * pack_tokens + first[:, :, None] + offsets[None, None, :]
    valid = offsets[None, None, :] < count[:, :, None]
    source = jnp.clip(source, 0, block.shape[0] - 1)
    picked = jnp.take(block, source.reshape(-1), axis=0)
    picked = picked.reshape(source.shape + (block.shape[1],))
    return jnp.where(valid[..., None], picked, jnp.zeros((), block.dtype))


def local(
    residual, partials, low_features, mid_features, join_weight, lengths, shard_of, joined_cotangent
):
    pack_tokens = low_features.shape[0]
    longest = pack_tokens // 4
    in_cols = residual.shape[1]
    shard_count = lax.axis_size("dp")
    tensor_count = lax.axis_size("tensor")
    packs_here = shard_count // tensor_count
    total = lax.psum(partials[0].astype(jnp.float32).astype(jnp.bfloat16), "tensor").astype(
        jnp.float32
    )
    own_sum = lax.dynamic_slice_in_dim(total, lax.axis_index("tensor") * in_cols, in_cols, 1)
    top_features = (residual.astype(jnp.float32) + own_sum).astype(jnp.bfloat16)
    stacked = jnp.stack([low_features, mid_features, top_features], axis=1)
    everyone = lax.all_gather(stacked, "dp", axis=0, tiled=True)
    rows = everyone
    joined_block = lax.psum_scatter(
        jnp.einsum("rki,kio->ro", rows, join_weight, preferred_element_type=jnp.float32),
        "tensor",
        scatter_dimension=0,
        tiled=True,
    ).astype(jnp.bfloat16)
    first_pack = lax.axis_index("tensor") * packs_here
    block_lengths = lax.dynamic_slice_in_dim(lengths, first_pack, packs_here, 0)
    block_shards = lax.dynamic_slice_in_dim(shard_of, first_pack, packs_here, 0)
    outgoing = build_slots(
        joined_block, block_lengths, block_shards, shard_count, longest, pack_tokens
    )
    routed_rows = lax.all_to_all(outgoing, "dp", split_axis=0, concat_axis=3, tiled=True)
    rows = everyone
    join_grad = jnp.einsum(
        "rki,ro->kio",
        rows,
        lax.all_gather(joined_cotangent, "tensor", axis=0, tiled=True),
        preferred_element_type=jnp.float32,
    )
    return (routed_rows, join_grad)


def solution(mesh):
    placed = (
        P("dp", "tensor"),
        P("tensor", "dp", None),
        P("dp", "tensor"),
        P("dp", "tensor"),
        P(None, "tensor", "dp"),
        P(),
        P(),
        P("tensor", "dp"),
    )
    return jax.shard_map(
        local,
        mesh=mesh,
        in_specs=placed,
        out_specs=(P("dp", "tensor", None, None), P(None, "tensor", "dp")),
        check_vma=False,
    )
```

profile of v0, /device:TPU:1, one launch (start us, length us, event | category | flops | bytes accessed | tf_op | source)
XLA Modules:
  0.0 267.6 jit_solution(12543434253317037843)
XLA Ops:
  7.2 0.0 all-reduce.2.cloned.1.call-start
  7.2 0.7 all-reduce.2.cloned.1.call-update
  7.9 0.0 all-gather.3.cloned.1.call-start
  8.0 69.3 %all-reduce.2.cloned.1.call-done = bf16[128,8192]{1,0:T(8,128)(2,1)} async-done(((bf16[128,8192]{1,0:T(8,128)(2,1)}), bf16[128,8192]{1,0:T(8,128)(2,1)}) %all-reduce.2.cloned.1.call-update) | async-done | bytes 2097168 | tf_op jit(solution)/shard_map/psum | solution.py:32
  77.3 1.1 fusion.2
  78.4 2.0 pad_maximum_fusion
  80.4 0.0 all-gather.3.cloned.1.call-update
  80.4 0.0 reduce-scatter.2.cloned.1.call-start
  80.4 91.8 %all-gather.3.cloned.1.call-done = bf16[2048,3,1024]{2,0,1:T(8,128)(2,1)} async-done(((bf16[128,3,1024]{2,0,1:T(8,128)(2,1)}), bf16[2048,3,1024]{2,0,1:T(8,128)(2,1)}) %all-gather.3.cloned.1.call-update) | async-done | bytes 12582928 | tf_op jit(solution)/shard_map/all_gather | solution.py:38
  172.2 10.9 %convolution_bitcast_fusion = f32[2048,512]{1,0:T(8,128)} fusion(bf16[2048,3,1024]{2,0,1:T(8,128)(2,1)} %all-gather.3.cloned.1.call-done, bf16[3,1024,512]{2,1,0:T(8,128)(2,1)S(1)} %copy-done), kind=kOutput, calls=%fused_computation.1 | convolution fusion | flops 6442450944 | bytes 19922944 | tf_op jit(solution)/shard_map/rki,kio->ro/dot_general | solution.py:41
  183.1 0.0 reduce-scatter.2.cloned.1.call-update
  183.2 0.0 all-gather.5.cloned.1.call-start
  183.2 0.5 all-gather.5.cloned.1.call-update
  183.7 0.1 copy-done.1
  183.8 0.0 copy-done.2
  183.8 0.1 constant_dynamic-slice_fusion
  183.9 0.1 select_reduce_fusion.1
  184.0 0.1 broadcast_add_fusion
  184.1 0.1 copy.16
  184.2 0.1 add_clamp_fusion
  184.3 0.1 min.12
  184.4 0.1 copy.15
  184.5 0.1 compare_and_fusion
  184.6 0.1 iota_compare_fusion
  184.7 33.2 %reduce-scatter.2.cloned.1.call-done = f32[256,512]{1,0:T(8,128)} async-done(((f32[2048,512]{1,0:T(8,128)}), f32[256,512]{1,0:T(8,128)}) %reduce-scatter.2.cloned.1.call-update) | async-done | bytes 524304 | tf_op jit(solution)/shard_map/reduce_scatter | solution.py:40
  217.9 1.1 convert_element_type.18
  219.0 5.1 %gather_fusion = bf16[1024,512]{1,0:T(8,128)(2,1)} fusion(bf16[256,512]{1,0:T(8,128)(2,1)S(1)} %convert_element_type.18, s32[1024]{0:T(1024)S(1)} %broadcast_clamp_fusion), kind=kCustom, calls=%fused_computation | custom fusion | bytes 2101248 | tf_op jit(solution)/shard_map/jit(_take)/gather | solution.py:18
  224.1 2.3 select_select_fusion
  226.3 6.6 %all-to-all-start = ((bf16[16,2,32,512]{3,2,1,0:T(8,128)(2,1)}), bf16[16,2,32,512]{3,2,1,0:T(8,128)(2,1)}, u32[]{:S(2)}, u32[]{:S(2)}) async-start(bf16[16,2,32,512]{3,2,1,0:T(8,128)(2,1)} %select_select_fusion), calls=%async_computation.1 | async-start | bytes 2097152 | tf_op jit(solution)/shard_map/all_to_all | solution.py:52
  232.9 13.9 %all-gather.5.cloned.1.call-done = bf16[2048,512]{1,0:T(8,128)(2,1)} async-done(((bf16[256,512]{1,0:T(8,128)(2,1)}), bf16[2048,512]{1,0:T(8,128)(2,1)}) %all-gather.5.cloned.1.call-update) | async-done | bytes 2097168 | tf_op jit(solution)/shard_map/all_gather | solution.py:57
  246.8 12.0 %fusion = f32[3,1024,512]{2,1,0:T(8,128)} fusion(bf16[2048,3,1024]{2,0,1:T(8,128)(2,1)} %all-gather.3.cloned.1.call-done, bf16[2048,512]{1,0:T(8,128)(2,1)} %all-gather.5.cloned.1.call-done), kind=kOutput, calls=%fused_computation.2 | convolution fusion | flops 6442450944 | bytes 20971520 | tf_op jit(solution)/shard_map/rki,ro->kio/dot_general | solution.py:54
  258.8 2.3 copy.20
  (10 shorter events, 0.1 us)
Async XLA Ops:
  7.2 165.0 %copy-start = (bf16[3,1024,512]{2,1,0:T(8,128)(2,1)S(1)}, bf16[3,1024,512]{2,1,0:T(8,128)(2,1)}, u32[]{:S(2)}) copy-start(bf16[3,1024,512]{2,1,0:T(8,128)(2,1)} %param.12) | copy-start | bytes 9437188
  7.2 70.1 %all-reduce.2.cloned.1.call-start = ((), (), s32[]{:S(2)}) async-start(), calls=%async_computation.2 | async-start | bytes 4194304 | tf_op jit(solution)/shard_map/psum | solution.py:32
  7.9 164.3 %all-gather.3.cloned.1.call-start = ((), (), s32[]{:S(2)}) async-start(), calls=%async_computation.3 | async-start | bytes 13369344 | tf_op jit(solution)/shard_map/all_gather | solution.py:38
  80.4 137.5 %reduce-scatter.2.cloned.1.call-start = ((), (), s32[]{:S(2)}) async-start(), calls=%async_computation.4 | async-start | bytes 4718592 | tf_op jit(solution)/shard_map/reduce_scatter | solution.py:40
  183.1 0.7 copy-start.1
  183.1 0.7 copy-start.2
  183.2 63.6 %all-gather.5.cloned.1.call-start = ((), (), s32[]{:S(2)}) async-start(), calls=%async_computation.5 | async-start | bytes 2359296 | tf_op jit(solution)/shard_map/all_gather | solution.py:57
  226.3 32.5 %all-to-all-start = ((bf16[16,2,32,512]{3,2,1,0:T(8,128)(2,1)}), bf16[16,2,32,512]{3,2,1,0:T(8,128)(2,1)}, u32[]{:S(2)}, u32[]{:S(2)}) async-start(bf16[16,2,32,512]{3,2,1,0:T(8,128)(2,1)} %select_select_fusion), calls=%async_computation.1 | async-start | bytes 2097152 | tf_op jit(solution)/shard_map/all_to_all | solution.py:52
Sparse Core Ops, SparseCore 0:
  10.4 66.8 all-reduce.1
  80.5 91.6 all-gather.2
  183.3 34.5 reduce-scatter.1
  219.5 27.2 all-gather.4
where the time goes:
time: 268 us
  waiting for transfers between devices  209 us (78%)
  matrix products  22.9 us (9%)
  between operations  13.8 us (5%)
  local copies, waits for them, and re-layouts  7.82 us (3%)
  other arithmetic  6.9 us (3%)
  starting transfers between devices  6.75 us (3%)
    all_gather x1, waiting for transfers between devices, local(): everyone = lax.all_gather(stacked, 'dp', axis=0, tiled=True)  91.8 us
    psum x1, waiting for transfers between devices, local(): lax.psum(partials[0].astype(jnp.float32).astype(jnp.bfloat16), 'tensor')  69.3 us
    reduce_scatter x1, waiting for transfers between devices, local(): lax.psum_scatter(jnp.einsum('rki,kio->ro', rows, join_weight, preferred_e...  33.2 us
    all_gather x1, waiting for transfers between devices, local(): lax.all_gather(joined_cotangent, 'tensor', axis=0, tiled=True)  13.9 us
    dot_general x1, matrix products, local(): jnp.einsum('rki,ro->kio', rows, lax.all_gather(joined_cotangent, 'tensor'...  12 us
    dot_general x1, matrix products, local(): jnp.einsum('rki,kio->ro', rows, join_weight, preferred_element_type=jnp.f...  10.9 us
    all_to_all x1, starting transfers between devices, local(): lax.all_to_all(outgoing, 'dp', split_axis=0, concat_axis=3, tiled=True)  6.59 us
  transfers between devices with their start and end apart: 5, of which 4 were waited for; matrix products, arithmetic and copies ran while one was open for 8% of the time, Pallas kernels for 0%

commit v1 on v0

v1 whole, which is shorter than its diff:
```python
import jax
import jax.numpy as jnp
from jax import lax
from jax.experimental import pallas as pl
from jax.experimental.pallas import tpu as pltpu
from jax.sharding import PartitionSpec as P

MESH = pl.DeviceIdType.MESH

KIND = (0, 1, 0, 1, 2, 0, 2, 1, 2, 0, 1, 2)
WAVE = (0, 0, 1, 1, 0, 2, 1, 2, 2, 3, 3, 3)
SLOTS = len(KIND)
FIRST_TOP = 4
NEXT = tuple(
    next((b2 for b2 in range(SLOTS) if KIND[b2] == KIND[b] and WAVE[b2] == WAVE[b] + 1), 0)
    for b in range(SLOTS)
)
CHUNKS = 4
GRAD_LAG = 6


def lut(values, index):
    out = jnp.int32(values[0])
    for i in range(1, len(values)):
        step = values[i] - values[i - 1]
        if step:
            out = out + jnp.where(index >= i, jnp.int32(step), jnp.int32(0))
    return out


def div(a, b):
    return lax.div(a, jnp.int32(b))


def rem(a, b):
    return lax.rem(a, jnp.int32(b))


def ring_position(ring, y, z):
    turn = rem(y + z, 4)
    return 4 * (y + div(ring, 2) * (z - y)) + turn


def ring_device(ring, position):
    u = div(position, 4)
    v = rem(rem(position, 4) - u + 8, 4)
    half = div(ring, 2)
    return 4 * (u + half * (v - u)) + (v + half * (u - v))


def kernel(
    residual, partials, low, mid, weight, cot, lengths, shards,
    routed, grad,
    blocks, w_buf, cot_buf, mate_buf, own_buf, sum_buf, x_buf, res_buf,
    joined, part_buf, owner_buf, slot_buf, select_buf, grad_buf,
    load_sem, mate_send, mate_recv, x_send, x_recv, ring_send, ring_recv,
    cot_send, cot_recv, part_send, part_recv, route_send, route_recv, grad_sem,
):
    d = lax.axis_index("dp")
    s = lax.axis_index("tensor")
    y, z = div(d, 4), rem(d, 4)
    x, core = div(s, 2), rem(s, 2)
    cls = rem(y + z, 4)

    ring_of = [
        rem(cls + a % 2, 2) + 2 * rem(div(cls, 2) + a // 2, 2) for a in range(4)
    ]
    sign_of = [1 - 2 * rem(ring, 2) for ring in ring_of]
    place_of = [ring_position(ring, y, z) for ring in ring_of]
    target_of = [
        ring_device(ring_of[a], rem(place_of[a] + sign_of[a] + 16, 16)) for a in range(4)
    ]

    def pack_of(a, wave):
        place = rem(place_of[a] - sign_of[a] * (4 * wave + a) + 32, 16)
        return ring_device(ring_of[a], place)

    def slot_of(pack):
        py, pz = div(pack, 4), rem(pack, 4)
        ring = rem(py + pz, 4)
        sign = 1 - 2 * rem(ring, 2)
        gap = rem(sign * (ring_position(ring, y, z) - ring_position(ring, py, pz)) + 32, 16)
        return div(gap, 4), rem(gap, 4)

    load_low = pltpu.make_async_copy(low, blocks.at[0, 0], load_sem.at[0])
    load_mid = pltpu.make_async_copy(mid, blocks.at[1, 0], load_sem.at[1])
    load_res = pltpu.make_async_copy(residual, res_buf, load_sem.at[2])
    load_w = pltpu.make_async_copy(weight, w_buf, load_sem.at[3])

    def columns(delta, which):
        chip = rem(x + delta, 4)
        start = pl.multiple_of((2 * chip + which) * 1024, 1024)
        return partials.at[0, :, pl.ds(start, 1024)]

    load_own = [
        pltpu.make_async_copy(columns(delta, core), own_buf.at[delta], load_sem.at[4 + delta])
        for delta in range(4)
    ]
    load_low.start()
    for delta in (2, 1, 3, 0):
        load_own[delta].start()
    load_mid.start()
    load_res.start()
    load_w.start()

    barrier = pltpu.get_barrier_semaphore()

    @pl.loop(1, 16)
    def _(step):
        pl.semaphore_signal(
            barrier, inc=1, device_id=(rem(d + step, 16), s), device_id_type=MESH
        )

    @pl.loop(1, 8)
    def _(step):
        pl.semaphore_signal(
            barrier, inc=1, device_id=(d, rem(s + step, 8)), device_id_type=MESH
        )

    for j in range(2):
        pack = 2 * s + j
        row = lax.broadcasted_iota(jnp.int32, (512, 128), 0)
        token = lax.broadcasted_iota(jnp.int32, (512, 128), 1)
        shard = jnp.right_shift(row, 5)
        offset = jnp.bitwise_and(row, 31)
        source = jnp.full((512, 128), -1, jnp.int32)
        start = jnp.int32(0)
        for conv in range(5):
            count = lengths[pack, conv]
            here = (shard == shards[pack, conv]) & (offset < count)
            source = jnp.where(here, start + offset, source)
            start = start + count
        select_buf[j] = jnp.where(source == token, 1.0, 0.0).astype(jnp.bfloat16)

    pl.semaphore_wait(barrier, 22)

    mate = (d, s + 1 - 2 * core)
    mate_copies = [
        pltpu.make_async_remote_copy(
            src_ref=columns(delta, 1 - core),
            dst_ref=mate_buf.at[delta],
            send_sem=mate_send.at[delta],
            recv_sem=mate_recv.at[delta],
            device_id=mate,
            device_id_type=MESH,
        )
        for delta in range(4)
    ]
    for delta in (2, 1, 3, 0):
        mate_copies[delta].start()

    def forward(a, b, chunk):
        rows = pl.ds(32 * chunk, 32)
        to_b, to_a = (b, a + 1) if a < 3 else (lut(NEXT, b), 0)
        pltpu.make_async_remote_copy(
            src_ref=blocks.at[b, a, rows],
            dst_ref=blocks.at[to_b, to_a, rows],
            send_sem=ring_send.at[a],
            recv_sem=ring_recv.at[to_b, to_a, chunk],
            device_id=(target_of[a], s),
            device_id_type=MESH,
        ).start()

    load_low.wait()
    for chunk in range(CHUNKS):
        forward(0, jnp.int32(0), chunk)
    load_mid.wait()
    for chunk in range(CHUNKS):
        forward(0, jnp.int32(1), chunk)

    x_copies = {}
    for delta in (2, 1, 3, 0):
        load_own[delta].wait()
        mate_copies[delta].wait_recv()
        sum_buf[delta] = (
            own_buf[delta].astype(jnp.float32) + mate_buf[delta].astype(jnp.float32)
        ).astype(jnp.bfloat16)
        if delta:
            x_copies[delta] = pltpu.make_async_remote_copy(
                src_ref=sum_buf.at[delta],
                dst_ref=x_buf.at[delta - 1],
                send_sem=x_send.at[delta - 1],
                recv_sem=x_recv.at[delta - 1],
                device_id=(d, 2 * rem(x + delta, 4) + core),
                device_id_type=MESH,
            )
            x_copies[delta].start()

    load_w.wait()
    load_res.wait()

    def own_top():
        for delta in (1, 2, 3):
            x_copies[delta].wait_recv()
        total = res_buf[...].astype(jnp.float32) + sum_buf[0].astype(jnp.float32)
        for delta in (1, 2, 3):
            total = total + x_buf[delta - 1].astype(jnp.float32)
        blocks[FIRST_TOP, 0] = total.astype(jnp.bfloat16)
        for chunk in range(CHUNKS):
            forward(0, jnp.int32(FIRST_TOP), chunk)
        for j in range(2):
            wave, stream = slot_of(2 * s + j)
            rows = cot.at[pl.ds(128 * j, 128)]
            pltpu.make_async_copy(rows, cot_buf.at[wave, stream], cot_recv).start()

            @pl.loop(1, 8)
            def _(step):
                pltpu.make_async_remote_copy(
                    src_ref=rows,
                    dst_ref=cot_buf.at[wave, stream],
                    send_sem=cot_send,
                    recv_sem=cot_recv,
                    device_id=(d, rem(s + step, 8)),
                    device_id_type=MESH,
                ).start()

    def handle(a, b, chunk):
        valid = (b >= 0) & (b < SLOTS)
        if a == 0:
            valid = valid & (b >= 2) & (b != FIRST_TOP)

        @pl.when(valid)
        def _():
            here = blocks.at[b, a, pl.ds(32 * chunk, 32)]
            pltpu.make_async_copy(here, here, ring_recv.at[b, a, chunk]).wait()
            if a < 3:
                forward(a, b, chunk)
            else:

                @pl.when(b < 9)
                def _():
                    forward(a, b, chunk)

    def joined_piece(b, kind, wave, piece):
        half, side = piece // 2, piece % 2
        rows = blocks[b, pl.ds(2 * half, 2)].reshape(256, 1024)
        product = jnp.dot(
            rows, w_buf[kind, :, pl.ds(256 * side, 256)], preferred_element_type=jnp.float32
        )
        at = (wave, pl.ds(256 * half, 256), pl.ds(256 * side, 256))
        joined[at] = jnp.where(kind == 0, 0.0, joined[at]) + product

    def grad_piece(b, piece):
        kind, wave = lut(KIND, b), lut(WAVE, b)
        rows = blocks[b, :, :, pl.ds(256 * piece, 256)].reshape(512, 256)
        product = lax.dot_general(
            rows,
            cot_buf[wave].reshape(512, 512),
            (((0,), (0,)), ((), ())),
            preferred_element_type=jnp.float32,
        )
        at = (kind, pl.ds(256 * piece, 256))
        grad_buf[at] = jnp.where(wave == 0, 0.0, grad_buf[at]) + product

    def send_parts(wave):
        for a in range(4):
            part_buf[wave, a] = joined[wave, pl.ds(128 * a, 128)].astype(jnp.bfloat16)
            pack = pack_of(a, wave)
            owner = div(pack, 2)
            there = owner_buf.at[rem(pack, 2), s]

            @pl.when(owner == s)
            def _():
                pltpu.make_async_copy(
                    part_buf.at[wave, a], there, part_recv.at[rem(pack, 2)]
                ).start()

            @pl.when(owner != s)
            def _():
                pltpu.make_async_remote_copy(
                    src_ref=part_buf.at[wave, a],
                    dst_ref=there,
                    send_sem=part_send,
                    recv_sem=part_recv.at[rem(pack, 2)],
                    device_id=(d, owner),
                    device_id_type=MESH,
                ).start()

    own_waves = [slot_of(2 * s + j)[0] for j in range(2)]

    def route(wave):
        for j in range(2):

            @pl.when(own_waves[j] == wave)
            def _():
                pltpu.make_async_copy(owner_buf.at[j], owner_buf.at[j], part_recv.at[j]).wait()
                total = owner_buf[j, 0].astype(jnp.float32)
                for t in range(1, 8):
                    total = total + owner_buf[j, t].astype(jnp.float32)
                slots = jnp.dot(
                    select_buf[j], total.astype(jnp.bfloat16), preferred_element_type=jnp.float32
                )
                slot_buf[j] = slots.astype(jnp.bfloat16).reshape(16, 32, 512)
                there = routed.at[0, j, :, pl.ds(pl.multiple_of(d * 512, 512), 512)]
                pltpu.make_async_copy(slot_buf.at[j, d], there, route_recv).start()

                @pl.loop(1, 16)
                def _(step):
                    shard = rem(d + step, 16)
                    pltpu.make_async_remote_copy(
                        src_ref=slot_buf.at[j, shard],
                        dst_ref=there,
                        send_sem=route_send,
                        recv_sem=route_recv,
                        device_id=(shard, s),
                        device_id_type=MESH,
                    ).start()

    def body(beta, carry):
        done = beta - 2
        kind, wave = lut(KIND, done), lut(WAVE, done)

        @pl.when(beta == FIRST_TOP)
        def _():
            own_top()

        @pl.when(beta == GRAD_LAG)
        def _():
            pltpu.make_async_copy(cot_buf, cot_buf, cot_recv).wait()

        for chunk in range(CHUNKS):
            for a in range(4):
                shift = chunk - 2 * a
                handle(a, beta + shift // CHUNKS, shift % CHUNKS)

            @pl.when(done >= 0)
            def _():
                joined_piece(done, kind, wave, chunk)

            @pl.when(beta >= GRAD_LAG)
            def _():
                grad_piece(beta - GRAD_LAG, chunk)

            if chunk == 0:
                @pl.when((beta == 7) | (beta == 9) | (beta == 11))
                def _():
                    route(div(beta - 7, 2))

        @pl.when((done >= 0) & (kind == 2))
        def _():
            send_parts(wave)

        return carry

    lax.fori_loop(0, SLOTS + 2, body, 0)

    def last(b, carry):
        for piece in range(4):
            grad_piece(b, piece)

        @pl.when(b >= 9)
        def _():
            kind = b - 9
            pltpu.make_async_copy(grad_buf.at[kind], grad.at[kind], grad_sem).start()

        return carry

    lax.fori_loop(SLOTS + 2 - GRAD_LAG, SLOTS, last, 0)
    route(jnp.int32(3))

    for delta in range(4):
        mate_copies[delta].wait_send()
    for delta in (1, 2, 3):
        x_copies[delta].wait_send()
    for a in range(4):
        sent = blocks.at[:, a] if a < 3 else blocks.at[pl.ds(0, 9), a]
        pltpu.make_async_copy(sent, sent, ring_send.at[a]).wait()
    sent = blocks.at[pl.ds(0, 7), 0]
    pltpu.make_async_copy(sent, sent, cot_send).wait()
    pltpu.make_async_copy(sent, sent, part_send).wait()
    pltpu.make_async_copy(grad_buf, grad_buf, grad_sem).wait()
    sent = slot_buf.at[:, pl.ds(0, 15)]
    pltpu.make_async_copy(sent, sent, route_send).wait()
    pltpu.make_async_copy(slot_buf, slot_buf, route_recv).wait()


def local(
    residual, partials, low_features, mid_features, join_weight, lengths, shard_of, joined_cotangent
):
    bf16, f32 = jnp.bfloat16, jnp.float32
    hbm = pl.BlockSpec(memory_space=pl.ANY)
    smem = pl.BlockSpec(memory_space=pltpu.SMEM)
    dma = pltpu.SemaphoreType.DMA
    return pl.pallas_call(
        kernel,
        out_shape=(
            jax.ShapeDtypeStruct((1, 2, 32, 8192), bf16),
            jax.ShapeDtypeStruct((3, 1024, 512), f32),
        ),
        in_specs=[hbm] * 6 + [smem] * 2,
        out_specs=(hbm, hbm),
        scratch_shapes=[
            pltpu.VMEM((SLOTS, 4, 128, 1024), bf16),
            pltpu.VMEM((3, 1024, 512), bf16),
            pltpu.VMEM((4, 4, 128, 512), bf16),
            pltpu.VMEM((4, 128, 1024), bf16),
            pltpu.VMEM((4, 128, 1024), bf16),
            pltpu.VMEM((4, 128, 1024), bf16),
            pltpu.VMEM((3, 128, 1024), bf16),
            pltpu.VMEM((128, 1024), bf16),
            pltpu.VMEM((4, 512, 512), f32),
            pltpu.VMEM((4, 4, 128, 512), bf16),
            pltpu.VMEM((2, 8, 128, 512), bf16),
            pltpu.VMEM((2, 16, 32, 512), bf16),
            pltpu.VMEM((2, 512, 128), bf16),
            pltpu.VMEM((3, 1024, 512), f32),
            dma((8,)),
            dma((4,)), dma((4,)),
            dma((3,)), dma((3,)),
            dma((4,)), dma((SLOTS, 4, CHUNKS)),
            dma, dma,
            dma, dma((2,)),
            dma, dma,
            dma,
        ],
        compiler_params=pltpu.CompilerParams(
            collective_id=0, has_side_effects=True, vmem_limit_bytes=56 * 1024 * 1024
        ),
    )(residual, partials, low_features, mid_features, join_weight, joined_cotangent, lengths, shard_of)


def solution(mesh):
    placed = (
        P("dp", "tensor"),
        P("tensor", "dp", None),
        P("dp", "tensor"),
        P("dp", "tensor"),
        P(None, "tensor", "dp"),
        P(),
        P(),
        P("tensor", "dp"),
    )
    return jax.shard_map(
        local,
        mesh=mesh,
        in_specs=placed,
        out_specs=(P("dp", "tensor", None, None), P(None, "tensor", "dp")),
        check_vma=False,
    )
```

time: 268 us -> 182 us (0.68)
  waiting for transfers between devices: 209 us -> 0 us
  Pallas kernels: 0 us -> 170 us
  matrix products: 22.9 us -> 0 us
  between operations: 13.8 us -> 0.64 us
  other arithmetic: 6.9 us -> 0 us
  starting transfers between devices: 6.75 us -> 0 us
  local copies, waits for them, and re-layouts: 7.82 us -> 11.2 us
    pallas_call x0 -> x1, Pallas kernels: none -> 170 us  [local(): pl.pallas_call(kernel, out_shape=(jax.ShapeDtypeStruct((1, 2, 32, 8192),...]
    all_gather x2 -> x0, waiting for transfers between devices: 106 us -> none  [the longest x1 91.8 us: local(): everyone = lax.all_gather(stacked, 'dp', axis=0, tiled=True)]
    psum x1 -> x0, waiting for transfers between devices: 69.3 us -> none  [local(): lax.psum(partials[0].astype(jnp.float32).astype(jnp.bfloat16), 'tensor')]
    reduce_scatter x1 -> x0, waiting for transfers between devices: 33.2 us -> none  [local(): lax.psum_scatter(jnp.einsum('rki,kio->ro', rows, join_weight, preferred_e...]
    dot_general x2 -> x0, matrix products: 22.9 us -> none  [the longest x1 12 us: local(): jnp.einsum('rki,ro->kio', rows, lax.all_gather(joined_cotangent, 'tensor'...]
    unnamed x6 -> x4, local copies, waits for them, and re-layouts: 0.11 us -> 11.2 us
    all_to_all x1 -> x0, starting transfers between devices: 6.59 us -> none  [local(): lax.all_to_all(outgoing, 'dp', split_axis=0, concat_axis=3, tiled=True)]
    gather x1 -> x0, local copies, waits for them, and re-layouts: 5.08 us -> none  [build_slots(): picked = jnp.take(block, source.reshape(-1), axis=0)]
  transfers between devices with their start and end apart: 5 -> 0, of which waited for: 4 -> 0; matrix products, arithmetic and copies ran while one was open for 8% -> 0% of each run, Pallas kernels for 0% -> 0%
where the time goes in v1:
time: 182 us
  Pallas kernels  170 us (93%)
  local copies, waits for them, and re-layouts  11.2 us (6%)
    pallas_call x1, Pallas kernels, local(): pl.pallas_call(kernel, out_shape=(jax.ShapeDtypeStruct((1, 2, 32, 8192),...  170 us
    unnamed x4, local copies, waits for them, and re-layouts  11.2 us

profile of v1, /device:TPU:1, one launch (start us, length us, event | category | flops | bytes accessed | tf_op | source)
XLA Modules:
  0.0 181.5 jit_solution(2746455231044205097)
XLA Ops:
  0.6 1.4 copy.10.lengths
  2.0 1.4 copy.11.shards
  3.4 169.7 %shard_map.95 = (bf16[1,2,32,8192]{3,2,1,0:T(8,128)(2,1)}, f32[3,1024,512]{2,1,0:T(8,128)}) custom-call(bf16[128,1024]{1,0:T(8,128)(2,1)} %residual.1, bf16[1,128,8192]{2,1,0:T(8,128)(2,1)} %partials.1, bf16[128,1024]{1,0:T(8,128)(2,1)} %low.1, bf16[128,1024]{1,0:T(8,128)(2,1)} %mid.1, bf16[3,1024,512]{2,1,0:T(8,128)(2,1)} %weight.1, bf16[256,512]{1,0:T(8,128)(2,1)} %cot.1, ...), custom_call_target="tpu_custom_call" | custom-call | tf_op jit(solution)/shard_map/pallas_call | solution.py:384
  173.1 2.3 %copy.14 = bf16[1,2,32,8192]{3,2,1,0:T(8,128)(2,1)} copy(bf16[1,2,32,8192]{3,2,1,0:T(8,128)(2,1)} %get-tuple-element.4) | data formatting | bytes 2097152
  175.3 6.2 %copy.15 = f32[3,1024,512]{2,1,0:T(8,128)} copy(f32[3,1024,512]{2,1,0:T(8,128)} %get-tuple-element.5) | data formatting | bytes 12582912

commit v2 on v1

v2 whole, which is shorter than its diff:
```python
import jax
import jax.numpy as jnp
from jax import lax
from jax.experimental import pallas as pl
from jax.experimental.pallas import tpu as pltpu
from jax.sharding import PartitionSpec as P

MESH = pl.DeviceIdType.MESH

FAR_SLOT = (0, 1, 3, 2)
LOW, MID, TOP = 0, 1, 2


def lut(values, index):
    out = jnp.int32(values[0])
    for i in range(1, len(values)):
        step = values[i] - values[i - 1]
        if step:
            out = out + jnp.where(index >= i, jnp.int32(step), jnp.int32(0))
    return out


def div(a, b):
    return lax.div(a, jnp.int32(b))


def rem(a, b):
    return lax.rem(a, jnp.int32(b))


def kernel(
    residual, partials, low, mid, weight, cot, lengths, shards,
    routed, grad,
    blocks, w_buf, cot_buf, mate_buf, own_buf, sum_buf, x_buf, res_buf,
    joined, part_buf, owner_buf, slot_buf, select_buf, grad_buf,
    load_sem, mate_send, mate_recv, x_send, x_recv, ring_send, ring_recv,
    cot_send, cot_recv, part_send, part_recv, route_send, route_recv, grad_sem,
):
    d = lax.axis_index("dp")
    s = lax.axis_index("tensor")
    y, z = div(d, 4), rem(d, 4)
    x, core = div(s, 2), rem(s, 2)

    def slot_of(pack):
        return (
            lut(FAR_SLOT, rem(div(pack, 4) - y + 4, 4)),
            lut(FAR_SLOT, rem(rem(pack, 4) - z + 4, 4)),
        )

    def pack_of(i, j):
        return 4 * rem(y + FAR_SLOT[i], 4) + rem(z + FAR_SLOT[j], 4)

    ahead = (4 * rem(y + 1, 4) + z, 4 * y + rem(z + 1, 4))
    behind = (4 * rem(y + 3, 4) + z, 4 * y + rem(z + 3, 4))

    class Move:
        def __init__(self, kind, axis, half, fixed, op):
            self.kind, self.axis, self.half, self.fixed, self.op = kind, axis, half, fixed, op

        def at(self, slot, first, count):
            rows = pl.ds(64 * self.half + first, count)
            if self.axis == 0:
                return blocks.at[self.kind, slot, self.fixed, rows]
            return blocks.at[self.kind, self.fixed, slot, rows]

        def send(self, src, dst, sem, device):
            pltpu.make_async_remote_copy(
                src_ref=src,
                dst_ref=dst,
                send_sem=ring_send.at[self.kind],
                recv_sem=ring_recv.at[self.kind, self.op, sem],
                device_id=(device, s),
                device_id_type=MESH,
            ).start()

        def wait(self, ref, sem):
            pltpu.make_async_copy(ref, ref, ring_recv.at[self.kind, self.op, sem]).wait()

        def start(self):
            self.send(self.at(0, 0, 64), self.at(2, 0, 64), 0, ahead[self.axis])
            self.send(self.at(0, 0, 64), self.at(1, 0, 64), 1, behind[self.axis])

        def relay_ahead(self):
            self.wait(self.at(2, 0, 64), 0)
            self.send(self.at(2, 0, 32), self.at(3, 0, 32), 2, ahead[self.axis])

        def relay_behind(self):
            self.wait(self.at(1, 0, 64), 1)
            self.send(self.at(1, 32, 32), self.at(3, 32, 32), 3, behind[self.axis])

        def finish(self):
            self.wait(self.at(3, 0, 32), 2)
            self.wait(self.at(3, 32, 32), 3)

    first_y = [Move(kind, 0, 0, 0, 0) for kind in range(3)]
    first_z = [Move(kind, 1, 1, 0, 1) for kind in range(3)]
    then_z = [[Move(kind, 1, 0, i, 2 + i) for i in range(4)] for kind in range(3)]
    then_y = [[Move(kind, 0, 1, j, 6 + j) for j in range(4)] for kind in range(3)]

    def begin(kind):
        first_y[kind].start()
        first_z[kind].start()
        then_z[kind][0].start()
        then_y[kind][0].start()

    def spread(kind):
        first_y[kind].relay_ahead()
        then_z[kind][2].start()
        first_z[kind].relay_ahead()
        then_y[kind][2].start()
        first_y[kind].relay_behind()
        then_z[kind][1].start()
        first_z[kind].relay_behind()
        then_y[kind][1].start()

    def far(kind):
        first_y[kind].finish()
        then_z[kind][3].start()
        first_z[kind].finish()
        then_y[kind][3].start()

    def relay(kind, slot):
        then_z[kind][slot].relay_ahead()
        then_y[kind][slot].relay_ahead()
        then_z[kind][slot].relay_behind()
        then_y[kind][slot].relay_behind()

    def finish(kind, slots):
        for slot in slots:
            then_z[kind][slot].finish()
            then_y[kind][slot].finish()

    load_low = pltpu.make_async_copy(low, blocks.at[LOW, 0, 0], load_sem.at[0])
    load_mid = pltpu.make_async_copy(mid, blocks.at[MID, 0, 0], load_sem.at[1])
    load_res = pltpu.make_async_copy(residual, res_buf, load_sem.at[2])
    load_w = pltpu.make_async_copy(weight, w_buf, load_sem.at[3])

    def columns(delta, which):
        chip = rem(x + delta, 4)
        start = pl.multiple_of((2 * chip + which) * 1024, 1024)
        return partials.at[0, :, pl.ds(start, 1024)]

    load_own = [
        pltpu.make_async_copy(columns(delta, core), own_buf.at[delta], load_sem.at[4 + delta])
        for delta in range(4)
    ]
    load_low.start()
    for delta in (2, 1, 3, 0):
        load_own[delta].start()
    load_mid.start()
    load_res.start()
    load_w.start()

    barrier = pltpu.get_barrier_semaphore()

    @pl.loop(1, 16)
    def _(step):
        pl.semaphore_signal(
            barrier, inc=1, device_id=(rem(d + step, 16), s), device_id_type=MESH
        )

    @pl.loop(1, 8)
    def _(step):
        pl.semaphore_signal(
            barrier, inc=1, device_id=(d, rem(s + step, 8)), device_id_type=MESH
        )

    for j in range(2):
        pack = 2 * s + j
        row = lax.broadcasted_iota(jnp.int32, (512, 128), 0)
        token = lax.broadcasted_iota(jnp.int32, (512, 128), 1)
        shard = jnp.right_shift(row, 5)
        offset = jnp.bitwise_and(row, 31)
        source = jnp.full((512, 128), -1, jnp.int32)
        start = jnp.int32(0)
        for conv in range(5):
            count = lengths[pack, conv]
            here = (shard == shards[pack, conv]) & (offset < count)
            source = jnp.where(here, start + offset, source)
            start = start + count
        select_buf[j] = jnp.where(source == token, 1.0, 0.0).astype(jnp.bfloat16)

    pl.semaphore_wait(barrier, 22)

    mate = (d, s + 1 - 2 * core)
    mate_copies = [
        pltpu.make_async_remote_copy(
            src_ref=columns(delta, 1 - core),
            dst_ref=mate_buf.at[delta],
            send_sem=mate_send.at[delta],
            recv_sem=mate_recv.at[delta],
            device_id=mate,
            device_id_type=MESH,
        )
        for delta in range(4)
    ]
    for delta in (2, 1, 3, 0):
        mate_copies[delta].start()

    load_low.wait()
    begin(LOW)
    load_mid.wait()
    begin(MID)

    x_copies = {}
    for delta in (2, 1, 3, 0):
        load_own[delta].wait()
        mate_copies[delta].wait_recv()
        sum_buf[delta] = (
            own_buf[delta].astype(jnp.float32) + mate_buf[delta].astype(jnp.float32)
        ).astype(jnp.bfloat16)
        if delta:
            x_copies[delta] = pltpu.make_async_remote_copy(
                src_ref=sum_buf.at[delta],
                dst_ref=x_buf.at[delta - 1],
                send_sem=x_send.at[delta - 1],
                recv_sem=x_recv.at[delta - 1],
                device_id=(d, 2 * rem(x + delta, 4) + core),
                device_id_type=MESH,
            )
            x_copies[delta].start()

    load_w.wait()
    load_res.wait()

    def own_top():
        for delta in (1, 2, 3):
            x_copies[delta].wait_recv()
        total = res_buf[...].astype(jnp.float32) + sum_buf[0].astype(jnp.float32)
        for delta in (1, 2, 3):
            total = total + x_buf[delta - 1].astype(jnp.float32)
        blocks[TOP, 0, 0] = total.astype(jnp.bfloat16)

    def send_cot():
        for j in range(2):
            slot_y, slot_z = slot_of(2 * s + j)
            rows = cot.at[pl.ds(128 * j, 128)]
            pltpu.make_async_copy(rows, cot_buf.at[slot_y, slot_z], cot_recv).start()

            @pl.loop(1, 8)
            def _(step):
                pltpu.make_async_remote_copy(
                    src_ref=rows,
                    dst_ref=cot_buf.at[slot_y, slot_z],
                    send_sem=cot_send,
                    recv_sem=cot_recv,
                    device_id=(d, rem(s + step, 8)),
                    device_id_type=MESH,
                ).start()

    def joined_all(kind):
        @pl.loop(0, 4)
        def _(i):
            rows = blocks[kind, i].reshape(512, 1024)
            for side in range(2):
                columns = pl.ds(256 * side, 256)
                product = jnp.dot(
                    rows, w_buf[kind, :, columns], preferred_element_type=jnp.float32
                ).reshape(4, 128, 256)
                at = (pl.ds(4 * i, 4), slice(None), columns)
                joined[at] = product if kind == LOW else joined[at] + product

    def grad_all(kind):
        @pl.loop(0, 4)
        def _(piece):
            features = pl.ds(pl.multiple_of(256 * piece, 256), 256)
            grad_buf[kind, features] = lax.dot_general(
                blocks[kind, :, :, :, features].reshape(2048, 256),
                cot_buf[...].reshape(2048, 512),
                (((0,), (0,)), ((), ())),
                preferred_element_type=jnp.float32,
            )

        pltpu.make_async_copy(grad_buf.at[kind], grad.at[kind], grad_sem.at[kind]).start()

    def send_part(i, j):
        pack = pack_of(i, j)
        owner = div(pack, 2)
        there = owner_buf.at[rem(pack, 2), s]

        @pl.when(owner == s)
        def _():
            pltpu.make_async_copy(part_buf.at[i, j], there, part_recv.at[rem(pack, 2)]).start()

        @pl.when(owner != s)
        def _():
            pltpu.make_async_remote_copy(
                src_ref=part_buf.at[i, j],
                dst_ref=there,
                send_sem=part_send,
                recv_sem=part_recv.at[rem(pack, 2)],
                device_id=(d, owner),
                device_id_type=MESH,
            ).start()

    def joined_top(i, j, ni, nj):
        count = ni * nj
        rows = blocks[TOP, i:i + ni, j:j + nj].reshape(128 * count, 1024)
        product = jnp.dot(rows, w_buf[TOP], preferred_element_type=jnp.float32)
        product = product.reshape(count, 128, 512)
        for n in range(count):
            at = (i + n // nj, j + n % nj)
            total = joined[4 * at[0] + at[1]] + product[n]
            part_buf[at] = total.astype(jnp.bfloat16)
            send_part(*at)

    own_far = []
    for j in range(2):
        slot_y, slot_z = slot_of(2 * s + j)
        own_far.append((slot_y == 3) | (slot_z == 3))

    def route(is_far):
        for j in range(2):

            @pl.when(own_far[j] if is_far else jnp.logical_not(own_far[j]))
            def _():
                pltpu.make_async_copy(owner_buf.at[j], owner_buf.at[j], part_recv.at[j]).wait()
                total = owner_buf[j, 0].astype(jnp.float32)
                for t in range(1, 8):
                    total = total + owner_buf[j, t].astype(jnp.float32)
                slots = jnp.dot(
                    select_buf[j], total.astype(jnp.bfloat16), preferred_element_type=jnp.float32
                )
                slot_buf[j] = slots.astype(jnp.bfloat16).reshape(16, 32, 512)
                there = routed.at[0, j, :, pl.ds(pl.multiple_of(d * 512, 512), 512)]
                pltpu.make_async_copy(slot_buf.at[j, d], there, route_recv).start()

                @pl.loop(1, 16)
                def _(step):
                    shard = rem(d + step, 16)
                    pltpu.make_async_remote_copy(
                        src_ref=slot_buf.at[j, shard],
                        dst_ref=there,
                        send_sem=route_send,
                        recv_sem=route_recv,
                        device_id=(shard, s),
                        device_id_type=MESH,
                    ).start()

    spread(LOW)
    spread(MID)
    far(LOW)
    relay(LOW, 0)
    far(MID)
    own_top()
    begin(TOP)
    send_cot()
    relay(MID, 0)
    relay(LOW, 2)
    relay(LOW, 1)
    relay(MID, 2)
    relay(MID, 1)
    relay(LOW, 3)
    relay(MID, 3)
    finish(LOW, range(4))
    spread(TOP)
    joined_all(LOW)
    far(TOP)
    finish(MID, range(4))
    joined_all(MID)
    relay(TOP, 0)
    pltpu.make_async_copy(cot_buf, cot_buf, cot_recv).wait()
    grad_all(LOW)
    relay(TOP, 2)
    relay(TOP, 1)
    for i in range(3):
        joined_top(i, 0, 1, 3)
    relay(TOP, 3)
    grad_all(MID)
    route(False)
    finish(TOP, range(3))
    joined_top(0, 3, 3, 1)
    finish(TOP, (3,))
    joined_top(3, 0, 1, 4)
    grad_all(TOP)
    route(True)

    for delta in range(4):
        mate_copies[delta].wait_send()
    for delta in (1, 2, 3):
        x_copies[delta].wait_send()
    for kind in range(3):
        sent = joined.at[pl.ds(0, 15)]
        pltpu.make_async_copy(sent, sent, ring_send.at[kind]).wait()
    sent = joined.at[pl.ds(0, 7)]
    pltpu.make_async_copy(sent, sent, cot_send).wait()
    pltpu.make_async_copy(sent, sent, part_send).wait()
    for kind in range(3):
        pltpu.make_async_copy(grad_buf.at[kind], grad.at[kind], grad_sem.at[kind]).wait()
    sent = slot_buf.at[:, pl.ds(0, 15)]
    pltpu.make_async_copy(sent, sent, route_send).wait()
    pltpu.make_async_copy(slot_buf, slot_buf, route_recv).wait()


def local(
    residual, partials, low_features, mid_features, join_weight, lengths, shard_of, joined_cotangent
):
    bf16, f32 = jnp.bfloat16, jnp.float32
    hbm = pl.BlockSpec(memory_space=pl.ANY)
    smem = pl.BlockSpec(memory_space=pltpu.SMEM)
    dma = pltpu.SemaphoreType.DMA
    return pl.pallas_call(
        kernel,
        out_shape=(
            jax.ShapeDtypeStruct((1, 2, 32, 8192), bf16),
            jax.ShapeDtypeStruct((3, 1024, 512), f32),
        ),
        in_specs=[hbm] * 6 + [smem] * 2,
        out_specs=(hbm, hbm),
        scratch_shapes=[
            pltpu.VMEM((3, 4, 4, 128, 1024), bf16),
            pltpu.VMEM((3, 1024, 512), bf16),
            pltpu.VMEM((4, 4, 128, 512), bf16),
            pltpu.VMEM((4, 128, 1024), bf16),
            pltpu.VMEM((4, 128, 1024), bf16),
            pltpu.VMEM((4, 128, 1024), bf16),
            pltpu.VMEM((3, 128, 1024), bf16),
            pltpu.VMEM((128, 1024), bf16),
            pltpu.VMEM((16, 128, 512), f32),
            pltpu.VMEM((4, 4, 128, 512), bf16),
            pltpu.VMEM((2, 8, 128, 512), bf16),
            pltpu.VMEM((2, 16, 32, 512), bf16),
            pltpu.VMEM((2, 512, 128), bf16),
            pltpu.VMEM((3, 1024, 512), f32),
            dma((8,)),
            dma((4,)), dma((4,)),
            dma((3,)), dma((3,)),
            dma((3,)), dma((3, 10, 4)),
            dma, dma,
            dma, dma((2,)),
            dma, dma,
            dma((3,)),
        ],
        compiler_params=pltpu.CompilerParams(
            collective_id=0, has_side_effects=True, vmem_limit_bytes=56 * 1024 * 1024
        ),
    )(residual, partials, low_features, mid_features, join_weight, joined_cotangent, lengths, shard_of)


def solution(mesh):
    placed = (
        P("dp", "tensor"),
        P("tensor", "dp", None),
        P("dp", "tensor"),
        P("dp", "tensor"),
        P(None, "tensor", "dp"),
        P(),
        P(),
        P("tensor", "dp"),
    )
    return jax.shard_map(
        local,
        mesh=mesh,
        in_specs=placed,
        out_specs=(P("dp", "tensor", None, None), P(None, "tensor", "dp")),
        check_vma=False,
    )
```

time: 182 us -> 142 us (0.78)
  Pallas kernels: 170 us -> 130 us
    pallas_call x1, Pallas kernels: 170 us -> 130 us  [local(): pl.pallas_call(kernel, out_shape=(jax.ShapeDtypeStruct((1, 2, 32, 8192),...]
where the time goes in v2:
time: 142 us; the launch traced here: 141 us
  Pallas kernels  130 us (92%)
  local copies, waits for them, and re-layouts  11.2 us (8%)
    pallas_call x1, Pallas kernels, local(): pl.pallas_call(kernel, out_shape=(jax.ShapeDtypeStruct((1, 2, 32, 8192),...  130 us
    unnamed x4, local copies, waits for them, and re-layouts  11.2 us

profile of v2, /device:TPU:1, one launch (start us, length us, event | category | flops | bytes accessed | tf_op | source)
XLA Modules:
  0.0 141.4 jit_solution(15821237840860870888)
XLA Ops:
  0.6 1.4 copy.10.lengths
  2.0 1.4 copy.11.shards
  3.4 129.6 %shard_map.95 = (bf16[1,2,32,8192]{3,2,1,0:T(8,128)(2,1)}, f32[3,1024,512]{2,1,0:T(8,128)}) custom-call(bf16[128,1024]{1,0:T(8,128)(2,1)} %residual.1, bf16[1,128,8192]{2,1,0:T(8,128)(2,1)} %partials.1, bf16[128,1024]{1,0:T(8,128)(2,1)} %low.1, bf16[128,1024]{1,0:T(8,128)(2,1)} %mid.1, bf16[3,1024,512]{2,1,0:T(8,128)(2,1)} %weight.1, bf16[256,512]{1,0:T(8,128)(2,1)} %cot.1, ...), custom_call_target="tpu_custom_call" | custom-call | tf_op jit(solution)/shard_map/pallas_call | solution.py:402
  133.0 2.3 %copy.14 = bf16[1,2,32,8192]{3,2,1,0:T(8,128)(2,1)} copy(bf16[1,2,32,8192]{3,2,1,0:T(8,128)(2,1)} %get-tuple-element.4) | data formatting | bytes 2097152
  135.2 6.2 %copy.15 = f32[3,1024,512]{2,1,0:T(8,128)} copy(f32[3,1024,512]{2,1,0:T(8,128)} %get-tuple-element.5) | data formatting | bytes 12582912

commit v3 on v2

--- a/solution.py
+++ b/solution.py
@@ -32,9 +32,9 @@
     residual, partials, low, mid, weight, cot, lengths, shards,
     routed, grad,
     blocks, w_buf, cot_buf, mate_buf, own_buf, sum_buf, x_buf, res_buf,
-    joined, part_buf, owner_buf, slot_buf, select_buf, grad_buf,
+    joined, part_buf, owner_buf, slot_buf, select_buf, grad_buf, plan_buf, mate_part,
     load_sem, mate_send, mate_recv, x_send, x_recv, ring_send, ring_recv,
-    cot_send, cot_recv, part_send, part_recv, route_send, route_recv, grad_sem,
+    cot_send, cot_recv, part_send, part_recv, pair_send, pair_recv, route_send, route_recv, grad_sem,
 ):
     d = lax.axis_index("dp")
     s = lax.axis_index("tensor")
@@ -113,9 +113,11 @@
         first_z[kind].relay_behind()
         then_y[kind][1].start()
 
-    def far(kind):
+    def far_z(kind):
         first_y[kind].finish()
         then_z[kind][3].start()
+
+    def far_y(kind):
         first_z[kind].finish()
         then_y[kind][3].start()
 
@@ -132,6 +134,8 @@
 
     load_low = pltpu.make_async_copy(low, blocks.at[LOW, 0, 0], load_sem.at[0])
     load_mid = pltpu.make_async_copy(mid, blocks.at[MID, 0, 0], load_sem.at[1])
+    load_lengths = pltpu.make_async_copy(lengths, plan_buf.at[0], load_sem.at[8])
+    load_shards = pltpu.make_async_copy(shards, plan_buf.at[1], load_sem.at[9])
     load_res = pltpu.make_async_copy(residual, res_buf, load_sem.at[2])
     load_w = pltpu.make_async_copy(weight, w_buf, load_sem.at[3])
 
@@ -145,6 +149,8 @@
         for delta in range(4)
     ]
     load_low.start()
+    load_lengths.start()
+    load_shards.start()
     for delta in (2, 1, 3, 0):
         load_own[delta].start()
     load_mid.start()
@@ -164,6 +170,9 @@
         pl.semaphore_signal(
             barrier, inc=1, device_id=(d, rem(s + step, 8)), device_id_type=MESH
         )
+
+    load_lengths.wait()
+    load_shards.wait()
 
     for j in range(2):
         pack = 2 * s + j
@@ -172,10 +181,12 @@
         shard = jnp.right_shift(row, 5)
         offset = jnp.bitwise_and(row, 31)
         source = jnp.full((512, 128), -1, jnp.int32)
-        start = jnp.int32(0)
+        start = jnp.zeros((1, 1), jnp.int32)
+        counts = plan_buf[0, pl.ds(pack, 1)]
+        places = plan_buf[1, pl.ds(pack, 1)]
         for conv in range(5):
-            count = lengths[pack, conv]
-            here = (shard == shards[pack, conv]) & (offset < count)
+            count = counts[:, conv:conv + 1]
+            here = (shard == places[:, conv:conv + 1]) & (offset < count)
             source = jnp.where(here, start + offset, source)
             start = start + count
         select_buf[j] = jnp.where(source == token, 1.0, 0.0).astype(jnp.bfloat16)
@@ -248,17 +259,24 @@
                     device_id_type=MESH,
                 ).start()
 
-    def joined_all(kind):
-        @pl.loop(0, 4)
+    def product_of(kind, i, j, ni, nj):
+        rows = blocks[kind, pl.ds(i, ni), j:j + nj].reshape(128 * ni * nj, 1024)
+        product = jnp.dot(rows, w_buf[kind], preferred_element_type=jnp.float32)
+        return product.reshape(ni, nj, 128, 512)
+
+    def joined_part(kind, i, j, ni, nj):
+        at = (pl.ds(i, ni), slice(j, j + nj))
+        product = product_of(kind, i, j, ni, nj)
+        joined[at] = product if kind == LOW else joined[at] + product
+
+    def joined_near(kind):
+        @pl.loop(0, 3)
         def _(i):
-            rows = blocks[kind, i].reshape(512, 1024)
-            for side in range(2):
-                columns = pl.ds(256 * side, 256)
-                product = jnp.dot(
-                    rows, w_buf[kind, :, columns], preferred_element_type=jnp.float32
-                ).reshape(4, 128, 256)
-                at = (pl.ds(4 * i, 4), slice(None), columns)
-                joined[at] = product if kind == LOW else joined[at] + product
+            joined_part(kind, i, 0, 1, 3)
+
+    def joined_far(kind):
+        joined_part(kind, 3, 0, 1, 3)
+        joined_part(kind, 0, 3, 4, 1)
 
     def grad_all(kind):
         @pl.loop(0, 4)
@@ -273,16 +291,39 @@
 
         pltpu.make_async_copy(grad_buf.at[kind], grad.at[kind], grad_sem.at[kind]).start()
 
+    def pair_part(i, j):
+        there = div(rem(pack_of(i, j), 4), 2)
+
+        @pl.when(there != core)
+        def _():
+            part_buf[i, j] = joined[i, j].astype(jnp.bfloat16)
+            pltpu.make_async_remote_copy(
+                src_ref=part_buf.at[i, j],
+                dst_ref=mate_part.at[i, j],
+                send_sem=pair_send,
+                recv_sem=pair_recv.at[i, j],
+                device_id=mate,
+                device_id_type=MESH,
+            ).start()
+
     def send_part(i, j):
         pack = pack_of(i, j)
         owner = div(pack, 2)
-        there = owner_buf.at[rem(pack, 2), s]
+        there = owner_buf.at[rem(pack, 2), x]
+
+        @pl.when(rem(owner, 2) == core)
+        def _():
+            pltpu.make_async_copy(
+                mate_part.at[i, j], mate_part.at[i, j], pair_recv.at[i, j]
+            ).wait()
+            total = joined[i, j] + mate_part[i, j].astype(jnp.float32)
+            part_buf[i, j] = total.astype(jnp.bfloat16)
 
         @pl.when(owner == s)
         def _():
             pltpu.make_async_copy(part_buf.at[i, j], there, part_recv.at[rem(pack, 2)]).start()
 
-        @pl.when(owner != s)
+        @pl.when((owner != s) & (rem(owner, 2) == core))
         def _():
             pltpu.make_async_remote_copy(
                 src_ref=part_buf.at[i, j],
@@ -293,30 +334,27 @@
                 device_id_type=MESH,
             ).start()
 
-    def joined_top(i, j, ni, nj):
-        count = ni * nj
-        rows = blocks[TOP, i:i + ni, j:j + nj].reshape(128 * count, 1024)
-        product = jnp.dot(rows, w_buf[TOP], preferred_element_type=jnp.float32)
-        product = product.reshape(count, 128, 512)
-        for n in range(count):
-            at = (i + n // nj, j + n % nj)
-            total = joined[4 * at[0] + at[1]] + product[n]
-            part_buf[at] = total.astype(jnp.bfloat16)
-            send_part(*at)
-
-    own_far = []
+    NEAR = [(i, j) for i in range(3) for j in range(3)]
+    FAR_ROW = [(3, j) for j in range(3)]
+    FAR_COLUMN = [(i, 3) for i in range(4)]
+
+    def each(f, packs):
+        for i, j in packs:
+            f(i, j)
+
+    own_group = []
     for j in range(2):
         slot_y, slot_z = slot_of(2 * s + j)
-        own_far.append((slot_y == 3) | (slot_z == 3))
-
-    def route(is_far):
+        own_group.append(jnp.where(slot_z == 3, 2, jnp.where(slot_y == 3, 1, 0)))
+
+    def route(group):
         for j in range(2):
 
-            @pl.when(own_far[j] if is_far else jnp.logical_not(own_far[j]))
+            @pl.when(own_group[j] == group)
             def _():
                 pltpu.make_async_copy(owner_buf.at[j], owner_buf.at[j], part_recv.at[j]).wait()
                 total = owner_buf[j, 0].astype(jnp.float32)
-                for t in range(1, 8):
+                for t in range(1, 4):
                     total = total + owner_buf[j, t].astype(jnp.float32)
                 slots = jnp.dot(
                     select_buf[j], total.astype(jnp.bfloat16), preferred_element_type=jnp.float32
@@ -339,52 +377,69 @@
 
     spread(LOW)
     spread(MID)
-    far(LOW)
-    relay(LOW, 0)
-    far(MID)
     own_top()
     begin(TOP)
     send_cot()
-    relay(MID, 0)
+    for kind in (LOW, MID):
+        relay(kind, 0)
     relay(LOW, 2)
     relay(LOW, 1)
+    joined_near(LOW)
+    spread(TOP)
     relay(MID, 2)
     relay(MID, 1)
-    relay(LOW, 3)
-    relay(MID, 3)
-    finish(LOW, range(4))
-    spread(TOP)
-    joined_all(LOW)
-    far(TOP)
-    finish(MID, range(4))
-    joined_all(MID)
+    far_z(LOW)
+    far_z(MID)
+    far_y(LOW)
+    joined_near(MID)
+    far_z(TOP)
     relay(TOP, 0)
-    pltpu.make_async_copy(cot_buf, cot_buf, cot_recv).wait()
-    grad_all(LOW)
     relay(TOP, 2)
     relay(TOP, 1)
-    for i in range(3):
-        joined_top(i, 0, 1, 3)
+    far_y(MID)
+    far_y(TOP)
+    joined_near(TOP)
+    each(pair_part, NEAR)
+    relay(LOW, 3)
+    each(send_part, NEAR)
+    finish(LOW, range(4))
+    joined_far(LOW)
+    relay(MID, 3)
+    pltpu.make_async_copy(cot_buf, cot_buf, cot_recv).wait()
+    finish(MID, range(4))
+    joined_far(MID)
     relay(TOP, 3)
+    route(0)
+    for slot in range(3):
+        then_y[TOP][slot].finish()
+    joined_part(TOP, 3, 0, 1, 3)
+    each(pair_part, FAR_ROW)
+    for slot in range(3):
+        then_z[TOP][slot].finish()
+    each(send_part, FAR_ROW)
+    finish(TOP, (3,))
+    joined_part(TOP, 0, 3, 4, 1)
+    each(pair_part, FAR_COLUMN)
+    grad_all(LOW)
+    each(send_part, FAR_COLUMN)
+    route(1)
     grad_all(MID)
-    route(False)
-    finish(TOP, range(3))
-    joined_top(0, 3, 3, 1)
-    finish(TOP, (3,))
-    joined_top(3, 0, 1, 4)
+    route(2)
     grad_all(TOP)
-    route(True)
+
+    def sent_bytes(count):
+        return joined.at[:, :, pl.ds(0, 8 * count)]
 
     for delta in range(4):
         mate_copies[delta].wait_send()
     for delta in (1, 2, 3):
         x_copies[delta].wait_send()
     for kind in range(3):
-        sent = joined.at[pl.ds(0, 15)]
+        sent = sent_bytes(15)
         pltpu.make_async_copy(sent, sent, ring_send.at[kind]).wait()
-    sent = joined.at[pl.ds(0, 7)]
-    pltpu.make_async_copy(sent, sent, cot_send).wait()
-    pltpu.make_async_copy(sent, sent, part_send).wait()
+    for count, sem in ((7, cot_send), (3, part_send), (4, pair_send)):
+        sent = sent_bytes(count)
+        pltpu.make_async_copy(sent, sent, sem).wait()
     for kind in range(3):
         pltpu.make_async_copy(grad_buf.at[kind], grad.at[kind], grad_sem.at[kind]).wait()
     sent = slot_buf.at[:, pl.ds(0, 15)]
@@ -397,7 +452,6 @@
 ):
     bf16, f32 = jnp.bfloat16, jnp.float32
     hbm = pl.BlockSpec(memory_space=pl.ANY)
-    smem = pl.BlockSpec(memory_space=pltpu.SMEM)
     dma = pltpu.SemaphoreType.DMA
     return pl.pallas_call(
         kernel,
@@ -405,7 +459,7 @@
             jax.ShapeDtypeStruct((1, 2, 32, 8192), bf16),
             jax.ShapeDtypeStruct((3, 1024, 512), f32),
         ),
-        in_specs=[hbm] * 6 + [smem] * 2,
+        in_specs=[hbm] * 8,
         out_specs=(hbm, hbm),
         scratch_shapes=[
             pltpu.VMEM((3, 4, 4, 128, 1024), bf16),
@@ -416,18 +470,21 @@
             pltpu.VMEM((4, 128, 1024), bf16),
             pltpu.VMEM((3, 128, 1024), bf16),
             pltpu.VMEM((128, 1024), bf16),
-            pltpu.VMEM((16, 128, 512), f32),
+            pltpu.VMEM((4, 4, 128, 512), f32),
             pltpu.VMEM((4, 4, 128, 512), bf16),
-            pltpu.VMEM((2, 8, 128, 512), bf16),
+            pltpu.VMEM((2, 4, 128, 512), bf16),
             pltpu.VMEM((2, 16, 32, 512), bf16),
             pltpu.VMEM((2, 512, 128), bf16),
             pltpu.VMEM((3, 1024, 512), f32),
-            dma((8,)),
+            pltpu.VMEM((2, 16, 5), jnp.int32),
+            pltpu.VMEM((4, 4, 128, 512), bf16),
+            dma((10,)),
             dma((4,)), dma((4,)),
             dma((3,)), dma((3,)),
             dma((3,)), dma((3, 10, 4)),
             dma, dma,
             dma, dma((2,)),
+            dma, dma((4, 4)),
             dma, dma,
             dma((3,)),
         ],

time: 142 us -> 117 us (0.82)
  Pallas kernels: 130 us -> 104 us
    pallas_call x1, Pallas kernels: 130 us -> 104 us  [local(): pl.pallas_call(kernel, out_shape=(jax.ShapeDtypeStruct((1, 2, 32, 8192),...]
where the time goes in v3:
time: 117 us; the launch traced here: 116 us
  Pallas kernels  104 us (89%)
  local copies, waits for them, and re-layouts  11.2 us (10%)
    pallas_call x1, Pallas kernels, local(): pl.pallas_call(kernel, out_shape=(jax.ShapeDtypeStruct((1, 2, 32, 8192),...  104 us
    unnamed x4, local copies, waits for them, and re-layouts  11.2 us

profile of v3, /device:TPU:1, one launch (start us, length us, event | category | flops | bytes accessed | tf_op | source)
XLA Modules:
  0.0 116.2 jit_solution(5870127914834224337)
XLA Ops:
  0.6 1.4 %copy.10.lengths = s32[16,5]{1,0:T(8,128)} copy(s32[16,5]{0,1:T(8,128)} %param.13) | data formatting | bytes 640 | tf_op args[5]
  2.0 1.4 %copy.11.shards = s32[16,5]{1,0:T(8,128)} copy(s32[16,5]{0,1:T(8,128)} %param.14) | data formatting | bytes 640 | tf_op args[6]
  3.4 104.4 %shard_map.95 = (bf16[1,2,32,8192]{3,2,1,0:T(8,128)(2,1)}, f32[3,1024,512]{2,1,0:T(8,128)}) custom-call(bf16[128,1024]{1,0:T(8,128)(2,1)} %residual.1, bf16[1,128,8192]{2,1,0:T(8,128)(2,1)} %partials.1, bf16[128,1024]{1,0:T(8,128)(2,1)} %low.1, bf16[128,1024]{1,0:T(8,128)(2,1)} %mid.1, bf16[3,1024,512]{2,1,0:T(8,128)(2,1)} %weight.1, bf16[256,512]{1,0:T(8,128)(2,1)} %cot.1, ...), custom_call_target="tpu_custom_call" | custom-call | tf_op jit(solution)/shard_map/pallas_call | solution.py:456
  107.7 2.3 %copy.14 = bf16[1,2,32,8192]{3,2,1,0:T(8,128)(2,1)} copy(bf16[1,2,32,8192]{3,2,1,0:T(8,128)(2,1)} %get-tuple-element.4) | data formatting | bytes 2097152
  110.0 6.2 %copy.15 = f32[3,1024,512]{2,1,0:T(8,128)} copy(f32[3,1024,512]{2,1,0:T(8,128)} %get-tuple-element.5) | data formatting | bytes 12582912

commit v4 on v3

--- a/solution.py
+++ b/solution.py
@@ -32,9 +32,9 @@
     residual, partials, low, mid, weight, cot, lengths, shards,
     routed, grad,
     blocks, w_buf, cot_buf, mate_buf, own_buf, sum_buf, x_buf, res_buf,
-    joined, part_buf, owner_buf, slot_buf, select_buf, grad_buf, plan_buf, mate_part,
+    joined, part_buf, owner_buf, slot_buf, select_buf, plan_buf, mate_part,
     load_sem, mate_send, mate_recv, x_send, x_recv, ring_send, ring_recv,
-    cot_send, cot_recv, part_send, part_recv, pair_send, pair_recv, route_send, route_recv, grad_sem,
+    cot_send, cot_recv, part_send, part_recv, pair_send, pair_recv, route_send, route_recv,
 ):
     d = lax.axis_index("dp")
     s = lax.axis_index("tensor")
@@ -182,11 +182,12 @@
         offset = jnp.bitwise_and(row, 31)
         source = jnp.full((512, 128), -1, jnp.int32)
         start = jnp.zeros((1, 1), jnp.int32)
-        counts = plan_buf[0, pl.ds(pack, 1)]
-        places = plan_buf[1, pl.ds(pack, 1)]
+        mine = lax.broadcasted_iota(jnp.int32, (5, 16), 1) == pack
+        counts = jnp.sum(jnp.where(mine, plan_buf[0], 0), axis=1, keepdims=True)
+        places = jnp.sum(jnp.where(mine, plan_buf[1], 0), axis=1, keepdims=True)
         for conv in range(5):
-            count = counts[:, conv:conv + 1]
-            here = (shard == places[:, conv:conv + 1]) & (offset < count)
+            count = counts[conv:conv + 1]
+            here = (shard == places[conv:conv + 1]) & (offset < count)
             source = jnp.where(here, start + offset, source)
             start = start + count
         select_buf[j] = jnp.where(source == token, 1.0, 0.0).astype(jnp.bfloat16)
@@ -282,14 +283,12 @@
         @pl.loop(0, 4)
         def _(piece):
             features = pl.ds(pl.multiple_of(256 * piece, 256), 256)
-            grad_buf[kind, features] = lax.dot_general(
+            grad[kind, features] = lax.dot_general(
                 blocks[kind, :, :, :, features].reshape(2048, 256),
                 cot_buf[...].reshape(2048, 512),
                 (((0,), (0,)), ((), ())),
                 preferred_element_type=jnp.float32,
             )
-
-        pltpu.make_async_copy(grad_buf.at[kind], grad.at[kind], grad_sem.at[kind]).start()
 
     def pair_part(i, j):
         there = div(rem(pack_of(i, j), 4), 2)
@@ -440,8 +439,6 @@
     for count, sem in ((7, cot_send), (3, part_send), (4, pair_send)):
         sent = sent_bytes(count)
         pltpu.make_async_copy(sent, sent, sem).wait()
-    for kind in range(3):
-        pltpu.make_async_copy(grad_buf.at[kind], grad.at[kind], grad_sem.at[kind]).wait()
     sent = slot_buf.at[:, pl.ds(0, 15)]
     pltpu.make_async_copy(sent, sent, route_send).wait()
     pltpu.make_async_copy(slot_buf, slot_buf, route_recv).wait()
@@ -452,15 +449,16 @@
 ):
     bf16, f32 = jnp.bfloat16, jnp.float32
     hbm = pl.BlockSpec(memory_space=pl.ANY)
+    vmem = pl.BlockSpec(memory_space=pltpu.VMEM)
     dma = pltpu.SemaphoreType.DMA
     return pl.pallas_call(
         kernel,
         out_shape=(
-            jax.ShapeDtypeStruct((1, 2, 32, 8192), bf16),
-            jax.ShapeDtypeStruct((3, 1024, 512), f32),
+            pltpu.VMEM((1, 2, 32, 8192), bf16),
+            pltpu.VMEM((3, 1024, 512), f32),
         ),
         in_specs=[hbm] * 8,
-        out_specs=(hbm, hbm),
+        out_specs=(vmem, vmem),
         scratch_shapes=[
             pltpu.VMEM((3, 4, 4, 128, 1024), bf16),
             pltpu.VMEM((3, 1024, 512), bf16),
@@ -475,8 +473,7 @@
             pltpu.VMEM((2, 4, 128, 512), bf16),
             pltpu.VMEM((2, 16, 32, 512), bf16),
             pltpu.VMEM((2, 512, 128), bf16),
-            pltpu.VMEM((3, 1024, 512), f32),
-            pltpu.VMEM((2, 16, 5), jnp.int32),
+            pltpu.VMEM((2, 5, 16), jnp.int32),
             pltpu.VMEM((4, 4, 128, 512), bf16),
             dma((10,)),
             dma((4,)), dma((4,)),
@@ -486,12 +483,11 @@
             dma, dma((2,)),
             dma, dma((4, 4)),
             dma, dma,
-            dma((3,)),
         ],
         compiler_params=pltpu.CompilerParams(
-            collective_id=0, has_side_effects=True, vmem_limit_bytes=56 * 1024 * 1024
+            collective_id=0, has_side_effects=True, vmem_limit_bytes=48 * 1024 * 1024
         ),
-    )(residual, partials, low_features, mid_features, join_weight, joined_cotangent, lengths, shard_of)
+    )(residual, partials, low_features, mid_features, join_weight, joined_cotangent, lengths.T, shard_of.T)
 
 
 def solution(mesh):

time: 117 us -> 109 us (0.932)
  local copies, waits for them, and re-layouts: 11.2 us -> 3.68 us
    unnamed x4 -> x2, local copies, waits for them, and re-layouts: 11.2 us -> 3.68 us
where the time goes in v4:
time: 109 us
  Pallas kernels  104 us (95%)
  local copies, waits for them, and re-layouts  3.68 us (3%)
    pallas_call x1, Pallas kernels, local(): pl.pallas_call(kernel, out_shape=(pltpu.VMEM((1, 2, 32, 8192), bf16), plt...  104 us
    unnamed x2, local copies, waits for them, and re-layouts  3.68 us

profile of v4, /device:TPU:1, one launch (start us, length us, event | category | flops | bytes accessed | tf_op | source)
XLA Modules:
  0.0 108.8 jit_solution(13265986939283990071)
XLA Ops:
  0.6 104.4 %shard_map.95 = (bf16[1,2,32,8192]{3,2,1,0:T(8,128)(2,1)S(1)}, f32[3,1024,512]{2,1,0:T(8,128)S(1)}) custom-call(bf16[128,1024]{1,0:T(8,128)(2,1)} %residual.1, bf16[1,128,8192]{2,1,0:T(8,128)(2,1)} %partials.1, bf16[128,1024]{1,0:T(8,128)(2,1)} %low.1, bf16[128,1024]{1,0:T(8,128)(2,1)} %mid.1, bf16[3,1024,512]{2,1,0:T(8,128)(2,1)} %weight.1, ...), custom_call_target="tpu_custom_call" | custom-call | tf_op jit(solution)/shard_map/pallas_call | solution.py:454
  105.1 1.0 copy.12
  106.1 2.7 %copy.13 = f32[3,1024,512]{2,1,0:T(8,128)} copy(f32[3,1024,512]{2,1,0:T(8,128)S(1)} %get-tuple-element.3) | data formatting | bytes 12582912

commit v5 on v4

--- a/solution.py
+++ b/solution.py
@@ -279,15 +279,29 @@
         joined_part(kind, 3, 0, 1, 3)
         joined_part(kind, 0, 3, 4, 1)
 
-    def grad_all(kind):
+    def grad_part(kind, features, i, ni, j, nj):
+        tokens = 128 * ni * nj
+        return lax.dot_general(
+            blocks[kind, i:i + ni, j:j + nj, :, features].reshape(tokens, 256),
+            cot_buf[i:i + ni, j:j + nj].reshape(tokens, 512),
+            (((0,), (0,)), ((), ())),
+            preferred_element_type=jnp.float32,
+        )
+
+    def grad_near(kind):
         @pl.loop(0, 4)
         def _(piece):
             features = pl.ds(pl.multiple_of(256 * piece, 256), 256)
-            grad[kind, features] = lax.dot_general(
-                blocks[kind, :, :, :, features].reshape(2048, 256),
-                cot_buf[...].reshape(2048, 512),
-                (((0,), (0,)), ((), ())),
-                preferred_element_type=jnp.float32,
+            grad[kind, features] = grad_part(kind, features, 0, 3, 0, 3)
+
+    def grad_far(kind):
+        @pl.loop(0, 4)
+        def _(piece):
+            features = pl.ds(pl.multiple_of(256 * piece, 256), 256)
+            grad[kind, features] = (
+                grad[kind, features]
+                + grad_part(kind, features, 3, 1, 0, 3)
+                + grad_part(kind, features, 0, 4, 3, 1)
             )
 
     def pair_part(i, j):
@@ -391,24 +405,24 @@
     far_z(MID)
     far_y(LOW)
     joined_near(MID)
-    far_z(TOP)
     relay(TOP, 0)
+    far_y(MID)
     relay(TOP, 2)
     relay(TOP, 1)
-    far_y(MID)
+    relay(LOW, 3)
+    far_z(TOP)
     far_y(TOP)
     joined_near(TOP)
     each(pair_part, NEAR)
-    relay(LOW, 3)
+    pltpu.make_async_copy(cot_buf, cot_buf, cot_recv).wait()
+    grad_near(LOW)
+    relay(MID, 3)
     each(send_part, NEAR)
     finish(LOW, range(4))
     joined_far(LOW)
-    relay(MID, 3)
-    pltpu.make_async_copy(cot_buf, cot_buf, cot_recv).wait()
+    relay(TOP, 3)
     finish(MID, range(4))
     joined_far(MID)
-    relay(TOP, 3)
-    route(0)
     for slot in range(3):
         then_y[TOP][slot].finish()
     joined_part(TOP, 3, 0, 1, 3)
@@ -419,12 +433,15 @@
     finish(TOP, (3,))
     joined_part(TOP, 0, 3, 4, 1)
     each(pair_part, FAR_COLUMN)
-    grad_all(LOW)
+    grad_near(TOP)
     each(send_part, FAR_COLUMN)
+    route(0)
     route(1)
-    grad_all(MID)
+    grad_near(MID)
+    grad_far(LOW)
+    grad_far(MID)
     route(2)
-    grad_all(TOP)
+    grad_far(TOP)
 
     def sent_bytes(count):
         return joined.at[:, :, pl.ds(0, 8 * count)]

time: 109 us -> 106 us (0.972)
  Pallas kernels: 104 us -> 101 us
    pallas_call x1, Pallas kernels: 104 us -> 101 us  [local(): pl.pallas_call(kernel, out_shape=(pltpu.VMEM((1, 2, 32, 8192), bf16), plt...]
where the time goes in v5:
time: 106 us; the launch traced here: 105 us
  Pallas kernels  101 us (95%)
  local copies, waits for them, and re-layouts  3.68 us (3%)
    pallas_call x1, Pallas kernels, local(): pl.pallas_call(kernel, out_shape=(pltpu.VMEM((1, 2, 32, 8192), bf16), plt...  101 us
    unnamed x2, local copies, waits for them, and re-layouts  3.68 us

profile of v5, /device:TPU:1, one launch (start us, length us, event | category | flops | bytes accessed | tf_op | source)
XLA Modules:
  0.0 105.5 jit_solution(12509004506981697781)
XLA Ops:
  0.6 101.1 %shard_map.95 = (bf16[1,2,32,8192]{3,2,1,0:T(8,128)(2,1)S(1)}, f32[3,1024,512]{2,1,0:T(8,128)S(1)}) custom-call(bf16[128,1024]{1,0:T(8,128)(2,1)} %residual.1, bf16[1,128,8192]{2,1,0:T(8,128)(2,1)} %partials.1, bf16[128,1024]{1,0:T(8,128)(2,1)} %low.1, bf16[128,1024]{1,0:T(8,128)(2,1)} %mid.1, bf16[3,1024,512]{2,1,0:T(8,128)(2,1)} %weight.1, ...), custom_call_target="tpu_custom_call" | custom-call | tf_op jit(solution)/shard_map/pallas_call | solution.py:471
  101.8 1.0 copy.12
  102.8 2.7 %copy.13 = f32[3,1024,512]{2,1,0:T(8,128)} copy(f32[3,1024,512]{2,1,0:T(8,128)S(1)} %get-tuple-element.3) | data formatting | bytes 12582912

commit v6 on v5

--- a/solution.py
+++ b/solution.py
@@ -121,16 +121,19 @@
         first_z[kind].finish()
         then_y[kind][3].start()
 
+    def relay_far(move):
+        move[3].relay_ahead()
+        move[3].relay_behind()
+
     def relay(kind, slot):
         then_z[kind][slot].relay_ahead()
         then_y[kind][slot].relay_ahead()
         then_z[kind][slot].relay_behind()
         then_y[kind][slot].relay_behind()
 
-    def finish(kind, slots):
-        for slot in slots:
-            then_z[kind][slot].finish()
-            then_y[kind][slot].finish()
+    def finish(moves):
+        for move in moves:
+            move.finish()
 
     load_low = pltpu.make_async_copy(low, blocks.at[LOW, 0, 0], load_sem.at[0])
     load_mid = pltpu.make_async_copy(mid, blocks.at[MID, 0, 0], load_sem.at[1])
@@ -275,10 +278,6 @@
         def _(i):
             joined_part(kind, i, 0, 1, 3)
 
-    def joined_far(kind):
-        joined_part(kind, 3, 0, 1, 3)
-        joined_part(kind, 0, 3, 4, 1)
-
     def grad_part(kind, features, i, ni, j, nj):
         tokens = 128 * ni * nj
         return lax.dot_general(
@@ -347,8 +346,7 @@
                 device_id_type=MESH,
             ).start()
 
-    NEAR = [(i, j) for i in range(3) for j in range(3)]
-    FAR_ROW = [(3, j) for j in range(3)]
+    NEAR = [(i, j) for i in range(4) for j in range(3)]
     FAR_COLUMN = [(i, 3) for i in range(4)]
 
     def each(f, packs):
@@ -358,7 +356,7 @@
     own_group = []
     for j in range(2):
         slot_y, slot_z = slot_of(2 * s + j)
-        own_group.append(jnp.where(slot_z == 3, 2, jnp.where(slot_y == 3, 1, 0)))
+        own_group.append(jnp.where(slot_z == 3, 1, 0))
 
     def route(group):
         for j in range(2):
@@ -407,40 +405,40 @@
     joined_near(MID)
     relay(TOP, 0)
     far_y(MID)
+    far_z(TOP)
     relay(TOP, 2)
     relay(TOP, 1)
-    relay(LOW, 3)
-    far_z(TOP)
     far_y(TOP)
     joined_near(TOP)
+    relay_far(then_z[LOW])
+    relay_far(then_z[MID])
+    finish(then_y[LOW][:3])
+    joined_part(LOW, 3, 0, 1, 3)
+    relay_far(then_z[TOP])
+    finish(then_y[MID][:3])
+    joined_part(MID, 3, 0, 1, 3)
+    finish(then_y[TOP][:3])
+    joined_part(TOP, 3, 0, 1, 3)
     each(pair_part, NEAR)
+    relay_far(then_y[LOW])
+    relay_far(then_y[MID])
+    each(send_part, NEAR)
+    relay_far(then_y[TOP])
     pltpu.make_async_copy(cot_buf, cot_buf, cot_recv).wait()
     grad_near(LOW)
-    relay(MID, 3)
-    each(send_part, NEAR)
-    finish(LOW, range(4))
-    joined_far(LOW)
-    relay(TOP, 3)
-    finish(MID, range(4))
-    joined_far(MID)
-    for slot in range(3):
-        then_y[TOP][slot].finish()
-    joined_part(TOP, 3, 0, 1, 3)
-    each(pair_part, FAR_ROW)
-    for slot in range(3):
-        then_z[TOP][slot].finish()
-    each(send_part, FAR_ROW)
-    finish(TOP, (3,))
+    for kind in (LOW, MID):
+        finish(then_z[kind] + then_y[kind][3:])
+        joined_part(kind, 0, 3, 4, 1)
+    finish(then_z[TOP] + then_y[TOP][3:])
     joined_part(TOP, 0, 3, 4, 1)
     each(pair_part, FAR_COLUMN)
-    grad_near(TOP)
     each(send_part, FAR_COLUMN)
     route(0)
+    grad_near(TOP)
+    grad_near(MID)
     route(1)
-    grad_near(MID)
     grad_far(LOW)
     grad_far(MID)
-    route(2)
     grad_far(TOP)
 
     def sent_bytes(count):

time: 106 us -> 99.8 us (0.942)
  Pallas kernels: 101 us -> 95.3 us
    pallas_call x1, Pallas kernels: 101 us -> 95.3 us  [local(): pl.pallas_call(kernel, out_shape=(pltpu.VMEM((1, 2, 32, 8192), bf16), plt...]
where the time goes in v6:
time: 99.8 us; the launch traced here: 99.6 us
  Pallas kernels  95.3 us (95%)
  local copies, waits for them, and re-layouts  3.68 us (4%)
    pallas_call x1, Pallas kernels, local(): pl.pallas_call(kernel, out_shape=(pltpu.VMEM((1, 2, 32, 8192), bf16), plt...  95.3 us
    unnamed x2, local copies, waits for them, and re-layouts  3.68 us

profile of v6, /device:TPU:1, one launch (start us, length us, event | category | flops | bytes accessed | tf_op | source)
XLA Modules:
  0.0 99.6 jit_solution(3788972240246103928)
XLA Ops:
  0.6 95.3 %shard_map.95 = (bf16[1,2,32,8192]{3,2,1,0:T(8,128)(2,1)S(1)}, f32[3,1024,512]{2,1,0:T(8,128)S(1)}) custom-call(bf16[128,1024]{1,0:T(8,128)(2,1)} %residual.1, bf16[1,128,8192]{2,1,0:T(8,128)(2,1)} %partials.1, bf16[128,1024]{1,0:T(8,128)(2,1)} %low.1, bf16[128,1024]{1,0:T(8,128)(2,1)} %mid.1, bf16[3,1024,512]{2,1,0:T(8,128)(2,1)} %weight.1, ...), custom_call_target="tpu_custom_call" | custom-call | tf_op jit(solution)/shard_map/pallas_call | solution.py:469
  96.0 1.0 copy.12
  96.9 2.7 %copy.13 = f32[3,1024,512]{2,1,0:T(8,128)} copy(f32[3,1024,512]{2,1,0:T(8,128)S(1)} %get-tuple-element.3) | data formatting | bytes 12582912
